TPU v7x, 32 devices: a whole 2x2x4 slice. The times are simulated.
32 devices in a mesh: tm: 8 (over y, x, core), col: 4 (over z).
Axes of the slice: x: 2, y: 2, z: 4, core: 2. Of those that a mesh axis runs over, the one named last changes fastest.
Arguments:
- panel: bfloat16 [1024, 131072], P('col', 'tm'), may hold values from -60 to 60
- response: float32 [131072], replicated, may hold values from 0.25 to 2.5
Outputs:
- normal: float32 [1024, 1024], P('col', 'tm')
All inputs are finite; a program needn't handle non-finite values.
Results may differ from a plain program's by a relative error of at most 0.0015.
Values may be sent and summed in bfloat16 or wider, within the bound.
A program may use at most 192 MiB of HBM per device.

v0:
```python
import math

import jax
import jax.numpy as jnp
from jax import lax
from jax.sharding import PartitionSpec as P

EPOCHS = 131072


def angle_tables(row_count, col_count, length):
    row_index = jnp.arange(row_count, dtype=jnp.int32)[:, None]
    col_index = jnp.arange(col_count, dtype=jnp.int32)[None, :]
    phase_index = row_index * col_index % length
    angle = phase_index.astype(jnp.float32) * (2.0 * math.pi / length)
    return (jnp.cos(angle), jnp.sin(angle))


def mixed(form, left, right):
    return jnp.einsum(form, left, right, precision=lax.Precision.HIGHEST)


def split_table(table):
    upper = table.astype(jnp.bfloat16)
    lower = (table - upper.astype(jnp.float32)).astype(jnp.bfloat16)
    return (upper, lower)


def exact_first(table, values):
    upper, lower = split_table(table)
    first = jnp.einsum("kja,jban->kbn", upper, values, preferred_element_type=jnp.float32)
    return first + jnp.einsum("kja,jban->kbn", lower, values, preferred_element_type=jnp.float32)


def whiten_series(series, tables):
    outer_cos, outer_sin, twist_cos, twist_sin, inner_cos, inner_sin, gain_grid = tables
    block_count, item_count, block_len = series.shape
    inner_len = inner_cos.shape[0]
    steps_per_block = block_len // inner_len
    outer_len = block_count * steps_per_block
    values = series.reshape(block_count, item_count, steps_per_block, inner_len)
    fold_cos = outer_cos.reshape(outer_len, block_count, steps_per_block)
    fold_sin = outer_sin.reshape(outer_len, block_count, steps_per_block)
    first_re = exact_first(fold_cos, values)
    first_im = -exact_first(fold_sin, values)
    turn_cos = twist_cos[:, None, :]
    turn_sin = twist_sin[:, None, :]
    turned_re = first_re * turn_cos + first_im * turn_sin
    turned_im = first_im * turn_cos - first_re * turn_sin
    spec_re = mixed("kbn,nl->kbl", turned_re, inner_cos) + mixed(
        "kbn,nl->kbl", turned_im, inner_sin
    )
    spec_im = mixed("kbn,nl->kbl", turned_im, inner_cos) - mixed(
        "kbn,nl->kbl", turned_re, inner_sin
    )
    weight = gain_grid[:, None, :]
    filt_re = spec_re * weight
    filt_im = spec_im * weight
    back_re = mixed("kbl,ln->kbn", filt_re, inner_cos) - mixed("kbl,ln->kbn", filt_im, inner_sin)
    back_im = mixed("kbl,ln->kbn", filt_im, inner_cos) + mixed("kbl,ln->kbn", filt_re, inner_sin)
    untw_re = back_re * turn_cos - back_im * turn_sin
    untw_im = back_im * turn_cos + back_re * turn_sin
    spread_cos = outer_cos.reshape(block_count, steps_per_block, outer_len)
    spread_sin = outer_sin.reshape(block_count, steps_per_block, outer_len)
    result = mixed("jak,kbn->jban", spread_cos, untw_re) - mixed(
        "jak,kbn->jban", spread_sin, untw_im
    )
    result = result * (1.0 / (outer_len * inner_len))
    return result.reshape(block_count, item_count, block_len).astype(jnp.bfloat16)


def on_device(panel, response):
    col_rows, epoch_count = panel.shape
    tm_count = lax.axis_size("tm")
    total_len = tm_count * epoch_count
    inner_len = math.gcd(256, epoch_count)
    outer_len = total_len // inner_len
    outer_cos, outer_sin = angle_tables(outer_len, outer_len, outer_len)
    twist_cos, twist_sin = angle_tables(outer_len, inner_len, total_len)
    inner_cos, inner_sin = angle_tables(inner_len, inner_len, inner_len)
    gain_grid = response.reshape(inner_len, outer_len).T
    tables = (outer_cos, outer_sin, twist_cos, twist_sin, inner_cos, inner_sin, gain_grid)
    grouped = panel.reshape(tm_count, col_rows // tm_count, epoch_count)
    filtered = whiten_series(
        lax.all_to_all(grouped, "tm", split_axis=0, concat_axis=0, tiled=True), tables
    )
    landed = lax.all_to_all(filtered, "tm", split_axis=0, concat_axis=0, tiled=True)
    whitened = landed.reshape(col_rows, epoch_count)
    partial_sum = lax.dot_general(
        whitened,
        lax.all_gather(whitened, "col", axis=0, tiled=True),
        (((1,), (1,)), ((), ())),
        preferred_element_type=jnp.float32,
    )
    summed = lax.psum_scatter(partial_sum, "tm", scatter_dimension=1, tiled=True)
    return summed / EPOCHS


def solution(mesh):
    in_specs = (P("col", "tm"), P())
    out_specs = P("col", "tm")
    return jax.shard_map(
        on_device, mesh=mesh, in_specs=in_specs, out_specs=out_specs, check_vma=False
    )
```

profile of v0, /device:TPU:0, one launch (start us, length us, event | category | flops | bytes accessed | tf_op | source)
XLA Modules:
  0.0 1228.4 jit_solution(11451510093979654870)
XLA Ops:
  6.5 5.3 all-to-all-start
  13.0 2.9 fusion.81
  15.9 90.5 %all-to-all-done = bf16[8,32,16384]{2,1,0:T(8,128)(2,1)} async-done(((bf16[8,32,16384]{2,1,0:T(8,128)(2,1)}), bf16[8,32,16384]{2,1,0:T(8,128)(2,1)}, u32[]{:S(2)}, u32[]{:S(2)}) %all-to-all-start) | async-done | bytes 8388640 | tf_op jit(solution)/shard_map/all_to_all | solution.py:85
  106.4 9.4 copy.17
  115.8 17.5 %fusion.12 = f32[512,32,256,1]{2,0,1,3:T(8,128)} fusion(s32[8,64]{1,0:T(8,128)S(1)} %multiply_add_fusion.3, bf16[8,32,64,256]{3,2,1,0:T(8,128)(2,1)} %bitcast.116), kind=kOutput, calls=%fused_computation.21 | convolution fusion | flops 4298899456 | bytes 25167872 | tf_op jit(solution)/shard_map/kja,jban->kbn/dot_general | solution.py:31
  133.3 14.1 %fusion.15 = f32[512,32,256,1]{2,0,1,3:T(8,128)} fusion(s32[8,64]{1,0:T(8,128)S(1)} %multiply_add_fusion.3, bf16[8,32,64,256]{3,2,1,0:T(8,128)(2,1)S(1)} %bitcast.119), kind=kOutput, calls=%fused_computation.24 | convolution fusion | flops 4298899456 | bytes 25167872 | tf_op jit(solution)/shard_map/kja,jban->kbn/dot_general | solution.py:31
  147.4 17.5 %fusion = f32[512,32,256]{2,0,1:T(8,128)} fusion(f32[512,32,256,1]{2,0,1,3:T(8,128)} %fusion.12, s32[8,64]{1,0:T(8,128)S(1)} %multiply_add_fusion.3, bf16[8,32,64,256]{3,2,1,0:T(8,128)(2,1)} %bitcast.117), kind=kOutput, calls=%fused_computation.1 | convolution fusion | flops 4308074496 | bytes 41945088 | tf_op jit(solution)/shard_map/kja,jban->kbn/dot_general | solution.py:32
  164.9 17.8 %bitcast_add_fusion.1 = f32[512,32,256]{2,0,1:T(8,128)} fusion(f32[512,32,256,1]{2,0,1,3:T(8,128)} %fusion.15, s32[8,64]{1,0:T(8,128)S(1)} %multiply_add_fusion.3, bf16[8,32,64,256]{3,2,1,0:T(8,128)(2,1)} %bitcast.118), kind=kOutput, calls=%fused_computation.2 | convolution fusion | flops 4303880192 | bytes 41945088 | tf_op jit(solution)/shard_map/kja,jban->kbn/dot_general | solution.py:32
  182.7 24.2 %fusion.25 = f32[512,32,256]{2,0,1:T(8,128)} fusion(f32[512,32,256]{2,0,1:T(8,128)} %bitcast_add_fusion.1, f32[512,32,256]{2,0,1:T(8,128)} %fusion, f32[512,256]{1,0:T(8,128)S(1)} %copy-done, f32[512,256]{1,0:T(8,128)S(1)} %copy-done.1), kind=kOutput, calls=%fused_computation.32 | convolution fusion | flops 12898402304 | bytes 51380224 | tf_op jit(solution)/shard_map/kbn,nl->kbl/dot_general | solution.py:20
  206.9 24.3 %fusion.24 = f32[512,32,256]{2,0,1:T(8,128)} fusion(f32[512,32,256]{2,0,1:T(8,128)} %fusion, f32[512,32,256]{2,0,1:T(8,128)} %bitcast_add_fusion.1, f32[512,256]{1,0:T(8,128)S(1)} %copy-done, f32[512,256]{1,0:T(8,128)S(1)} %copy-done.1), kind=kOutput, calls=%fused_computation.31 | convolution fusion | flops 12898402304 | bytes 51380224 | tf_op jit(solution)/shard_map/kbn,nl->kbl/dot_general | solution.py:20
  231.2 29.4 %subtract_multiply_fusion = f32[512,32,256]{2,0,1:T(8,128)} fusion(f32[512,32,256]{2,0,1:T(8,128)} %fusion.25, f32[512,256]{1,0:T(8,128)S(1)} %copy-done.3, f32[512,32,256]{2,0,1:T(8,128)} %fusion, f32[512,32,256]{2,0,1:T(8,128)} %bitcast_add_fusion.1, f32[512,256]{1,0:T(8,128)S(1)} %copy-done, f32[512,256]{1,0:T(8,128)S(1)} %copy-done.1), kind=kOutput, calls=%fused_computation.14 | convolution fusion | flops 12906790912 | bytes 68681728 | tf_op jit(solution)/shard_map/kbn,nl->kbl/dot_general | solution.py:20
  260.6 22.0 %fusion.73 = f32[512,32,256]{2,0,1:T(8,128)} fusion(f32[512,32,256]{2,0,1:T(8,128)} %subtract_multiply_fusion), kind=kOutput, calls=%fused_computation.84 | convolution fusion | flops 12885819392 | bytes 33554432 | tf_op jit(solution)/shard_map/kbl,ln->kbn/dot_general | solution.py:20
  282.5 29.4 %add_multiply_fusion = f32[512,32,256]{2,0,1:T(8,128)} fusion(f32[512,32,256]{2,0,1:T(8,128)} %fusion.24, f32[512,256]{1,0:T(8,128)S(1)} %copy-done.3, f32[512,32,256]{2,0,1:T(8,128)} %bitcast_add_fusion.1, f32[512,32,256]{2,0,1:T(8,128)} %fusion, f32[512,256]{1,0:T(8,128)S(1)} %copy-done, f32[512,256]{1,0:T(8,128)S(1)} %copy-done.1), kind=kOutput, calls=%fused_computation.15 | convolution fusion | flops 12906790912 | bytes 68681728 | tf_op jit(solution)/shard_map/kbn,nl->kbl/dot_general | solution.py:20
  311.9 22.2 %fusion.76 = f32[512,32,256]{2,0,1:T(8,128)} fusion(f32[512,32,256]{2,0,1:T(8,128)} %add_multiply_fusion), kind=kOutput, calls=%fused_computation.87 | convolution fusion | flops 12885819392 | bytes 33554432 | tf_op jit(solution)/shard_map/kbl,ln->kbn/dot_general | solution.py:20
  334.1 23.7 %convolution_add_fusion = f32[512,32,256]{2,0,1:T(8,128)} fusion(f32[512,32,256]{2,0,1:T(8,128)} %fusion.73, f32[512,32,256]{2,0,1:T(8,128)} %add_multiply_fusion), kind=kOutput, calls=%fused_computation.18 | convolution fusion | flops 12890013696 | bytes 50331648 | tf_op jit(solution)/shard_map/kbl,ln->kbn/dot_general | solution.py:20
  357.8 23.7 %convolution_subtract_fusion = f32[512,32,256]{2,0,1:T(8,128)} fusion(f32[512,32,256]{2,0,1:T(8,128)} %fusion.76, f32[512,32,256]{2,0,1:T(8,128)} %subtract_multiply_fusion), kind=kOutput, calls=%fused_computation.19 | convolution fusion | flops 12890013696 | bytes 50331648 | tf_op jit(solution)/shard_map/kbl,ln->kbn/dot_general | solution.py:20
  381.5 48.6 %fusion.1 = f32[32,256,8,64]{1,3,2,0:T(8,128)} fusion(f32[512,32,256]{2,0,1:T(8,128)} %convolution_subtract_fusion, f32[512,32,256]{2,0,1:T(8,128)} %convolution_add_fusion, f32[512,256]{1,0:T(8,128)S(1)} %copy-done, f32[512,256]{1,0:T(8,128)S(1)} %copy-done.1, s32[8,64]{1,0:T(8,128)S(1)} %multiply_add_fusion.3), kind=kOutput, calls=%fused_computation.3 | convolution fusion | flops 25786056704 | bytes 51382272 | tf_op jit(solution)/shard_map/jak,kbn->jban/dot_general | solution.py:20
  430.1 51.6 %fusion.11 = bf16[8,32,64,256]{3,2,0,1:T(8,128)(2,1)} fusion(f32[32,256,8,64]{1,3,2,0:T(8,128)} %fusion.1, f32[512,32,256]{2,0,1:T(8,128)} %convolution_add_fusion, f32[512,32,256]{2,0,1:T(8,128)} %convolution_subtract_fusion, f32[512,256]{1,0:T(8,128)S(1)} %copy-done, f32[512,256]{1,0:T(8,128)S(1)} %copy-done.1, s32[8,64]{1,0:T(8,128)S(1)} %multiply_add_fusion.3), kind=kOutput, calls=%fused_computation.20 | convolution fusion | flops 25798639616 | bytes 59770880 | tf_op jit(solution)/shard_map/jak,kbn->jban/dot_general | solution.py:20
  481.8 13.5 %convert_element_type.101 = bf16[8,32,16384]{2,0,1:T(8,128)(2,1)} reshape(bf16[8,32,64,256]{3,2,0,1:T(8,128)(2,1)} %fusion.11) | data formatting | bytes 16777216 | tf_op jit(solution)/shard_map/convert_element_type | solution.py:69
  495.3 11.2 copy.9
  506.5 99.7 %all_to_all.10 = bf16[8,32,16384]{2,1,0:T(8,128)(2,1)} all-to-all(bf16[8,32,16384]{2,1,0:T(8,128)(2,1)} %copy.9), channel_id=1, replica_groups=mesh['tm'=8,'col'=4] {'tm'}, dimensions={0} | all-to-all | bytes 16777216 | tf_op jit(solution)/shard_map/all_to_all | solution.py:87
  606.3 561.6 %all-gather.2.cloned.1.call-done = bf16[1024,16384]{1,0:T(8,128)(2,1)} async-done(((bf16[256,16384]{1,0:T(8,128)(2,1)}), bf16[1024,16384]{1,0:T(8,128)(2,1)}) %all-gather.2.cloned.1.call-update) | async-done | bytes 33554448 | tf_op jit(solution)/shard_map/all_gather | solution.py:91
  1167.9 17.5 %fusion.150 = f32[256,1024]{1,0:T(8,128)} fusion(bf16[256,16384]{1,0:T(8,128)(2,1)} %bitcast.114, bf16[1024,16384]{1,0:T(8,128)(2,1)} %all-gather.2.cloned.1.call-done), kind=kOutput, calls=%fused_computation.155 | convolution fusion | flops 8589934592 | bytes 42991616 | tf_op jit(solution)/shard_map/dot_general | solution.py:89
  1185.4 34.4 %reduce-scatter.2.cloned.1.call-done = f32[256,128]{1,0:T(8,128)} async-done(((f32[256,1024]{1,0:T(8,128)}), f32[256,128]{1,0:T(8,128)}) %reduce-scatter.2.cloned.1.call-update) | async-done | bytes 131088 | tf_op jit(solution)/shard_map/reduce_scatter | solution.py:95
  (18 shorter events, 2.8 us)
Async XLA Ops:
  6.5 5.4 copy-start.4
  6.5 99.8 %all-to-all-start = ((bf16[8,32,16384]{2,1,0:T(8,128)(2,1)}), bf16[8,32,16384]{2,1,0:T(8,128)(2,1)}, u32[]{:S(2)}, u32[]{:S(2)}) async-start(bf16[8,32,16384]{2,1,0:T(8,128)(2,1)} %bitcast.115), calls=%async_computation | async-start | bytes 16777216 | tf_op jit(solution)/shard_map/all_to_all | solution.py:85
  11.8 1156.1 %all-gather.2.cloned.1.call-start = ((), (), s32[]{:S(2)}) async-start(), calls=%async_computation.3 | async-start | bytes 41943040 | tf_op jit(solution)/shard_map/all_gather | solution.py:91
  115.8 17.6 %copy-start.2 = (bf16[32,8,64,256]{3,2,1,0:T(8,128)(2,1)S(1)}, bf16[32,8,64,256]{3,2,1,0:T(8,128)(2,1)}, u32[]{:S(2)}) copy-start(bf16[32,8,64,256]{3,2,1,0:T(8,128)(2,1)} %copy.17) | copy-start | bytes 25165828
  164.9 17.8 %copy-start = (f32[512,256]{1,0:T(8,128)S(1)}, f32[512,256]{1,0:T(8,128)}, u32[]{:S(2)}) copy-start(f32[512,256]{1,0:T(8,128)} %get-tuple-element.5) | copy-start | bytes 1572868
  164.9 17.8 %copy-start.1 = (f32[512,256]{1,0:T(8,128)S(1)}, f32[512,256]{1,0:T(8,128)}, u32[]{:S(2)}) copy-start(f32[512,256]{1,0:T(8,128)} %get-tuple-element.6) | copy-start | bytes 1572868
  206.9 24.3 %copy-start.3 = (f32[512,256]{1,0:T(8,128)S(1)}, f32[512,256]{1,0:T(8,128)}, u32[]{:S(2)}) copy-start(f32[512,256]{1,0:T(8,128)} %copy.8) | copy-start | bytes 1572868
  606.2 613.6 %reduce-scatter.2.cloned.1.call-start = ((), (), s32[]{:S(2)}) async-start(), calls=%async_computation.4 | async-start | bytes 1179648 | tf_op jit(solution)/shard_map/reduce_scatter | solution.py:95
Sparse Core Ops, SparseCore 0:
  606.4 561.5 all-gather.1
  1185.5 34.2 reduce-scatter.1
where the time goes:
time: 1240 us; the launch traced here: 1230 us
  waiting for transfers between devices  687 us (55%)
  matrix products  383 us (31%)
  blocking collectives  99.7 us (8%)
  local copies, waits for them, and re-layouts  35.2 us (3%)
  between operations  13.6 us (1%)
    all_gather x1, waiting for transfers between devices, on_device(): lax.all_gather(whitened, 'col', axis=0, tiled=True)  562 us
    dot_general x10, matrix products, mixed(): return jnp.einsum(form, left, right, precision=lax.Precision.HIGHEST)  299 us
    all_to_all x1, blocking collectives, on_device(): lax.all_to_all(filtered, 'tm', split_axis=0, concat_axis=0, tiled=True)  99.7 us
    all_to_all x1, waiting for transfers between devices, on_device(): lax.all_to_all(grouped, 'tm', split_axis=0, concat_axis=0, tiled=True)  90.5 us
    dot_general x2, matrix products, exact_first(): jnp.einsum('kja,jban->kbn', lower, values, preferred_element_type=jnp.flo...  35.3 us
    reduce_scatter x1, waiting for transfers between devices, on_device(): lax.psum_scatter(partial_sum, 'tm', scatter_dimension=1, tiled=True)  34.4 us
    dot_general x2, matrix products, exact_first(): jnp.einsum('kja,jban->kbn', upper, values, preferred_element_type=jnp.flo...  31.6 us
  transfers between devices with their start and end apart: 3, of which 3 were waited for; matrix products, arithmetic and copies ran while one was open for 0% of the time, Pallas kernels for 0%

commit v1 on v0

v1 whole, which is shorter than its diff:
```python
import functools
import math

import jax
import jax.numpy as jnp
import numpy as np
from jax import lax
from jax.experimental import pallas as pl
from jax.experimental.pallas import tpu as pltpu
from jax.sharding import PartitionSpec as P

INNER = 256
LANES = 128
VMEM_BYTES = 58 * 1024 * 1024


def split_table(table):
    upper = np.asarray(table, np.float32).astype(jnp.bfloat16)
    lower = (np.asarray(table, np.float64) - upper.astype(np.float64)).astype(jnp.bfloat16)
    return np.stack([upper, lower])


def make_tables(total_len):
    outer = total_len // INNER
    half = outer // 2
    row = np.arange(half)[:, None]
    angle = 2.0 * math.pi * (row * np.arange(outer)[None, :] % outer) / outer
    cosine, sine = np.cos(angle), -np.sin(angle)
    sine[0] = 1.0 - 2.0 * (np.arange(outer) % 2)
    first = split_table(np.concatenate([cosine, sine]))
    lane = np.arange(INNER)
    angle = 2.0 * math.pi * (row * lane[None, :] % total_len) / total_len
    twist = np.stack([np.cos(angle), np.sin(angle)]).astype(np.float32)
    angle = 2.0 * math.pi * (lane[:, None] * lane[None, :] % INNER) / INNER
    cosine, sine = np.cos(angle), np.sin(angle)
    inner = split_table(np.block([[cosine, -sine], [sine, cosine]]))
    back = split_table(np.block([[cosine, sine], [-sine, cosine]]))
    return first, twist, inner, back


def gain_tables(response, total_len):
    outer = total_len // INNER
    half = outer // 2
    mirrored = jnp.concatenate([response[:1], jnp.flip(response[1:])])
    gain = 0.5 * (response + mirrored)
    grid = gain.reshape(INNER, outer).T
    wide = jnp.tile(grid[:half] * (math.sqrt(2.0) / INNER), (1, 2))
    lane = np.arange(INNER)
    blocks = []
    for shift, channel in ((0, 0), (1, half)):
        angle = math.pi * (lane[:, None] * (2 * lane[None, :] + shift) % (2 * INNER)) / INNER
        basis = np.concatenate([np.cos(angle), np.sin(angle)], axis=1).astype(np.float32)
        scaled = basis * jnp.tile(grid[channel] / INNER, 2)[None, :]
        blocks.append(jnp.dot(scaled, basis.T, precision=lax.Precision.HIGHEST))
    zero = jnp.zeros_like(blocks[0])
    edge = jnp.concatenate(
        [jnp.concatenate([blocks[0], zero], axis=1), jnp.concatenate([zero, blocks[1]], axis=1)]
    )
    upper = edge.astype(jnp.bfloat16)
    lower = (edge - upper.astype(jnp.float32)).astype(jnp.bfloat16)
    return wide, jnp.stack([upper, lower])


def product(left, right):
    return jnp.dot(left, right, preferred_element_type=jnp.float32)


def outer_stage(values, first, twist, mixed, index, count):
    half = twist.shape[1]
    sums = product(first[0], values) + product(first[1], values)
    real, imag = sums[:half], sums[half:]
    cosine, sine = twist[0], twist[1]
    turned = (real * cosine + imag * sine, imag * cosine - real * sine)
    for piece in range(2 * INNER // LANES):
        part, lane = divmod(piece * LANES, INNER)
        mixed.at[piece][pl.ds(index, half, stride=count), :] = turned[part][:, lane : lane + LANES]


def mixed_rows(mixed, start, size):
    return jnp.concatenate([mixed[piece, pl.ds(start, size), :] for piece in range(mixed.shape[0])], axis=1)


def inner_stage(values, gain, inner, back):
    rows = values.astype(jnp.bfloat16)
    spectrum = product(rows, inner[0]) + product(rows, inner[1])
    channels = gain.shape[0]
    spectrum = spectrum.reshape(channels, -1, 2 * INNER) * gain[:, None, :]
    spectrum = spectrum.reshape(-1, 2 * INNER)
    upper = spectrum.astype(jnp.bfloat16)
    lower = (spectrum - upper.astype(jnp.float32)).astype(jnp.bfloat16)
    return product(upper, back[0]) + product(lower, back[0]) + product(upper, back[1])


def edge_stage(values, edge):
    rows = values.astype(jnp.bfloat16)
    return product(rows, edge[0]) + product(rows, edge[1])


def filter_kernel(panel_ref, first_ref, twist_ref, inner_ref, back_ref, gain_ref, edge_ref, out_ref, mixed):
    sources, count, steps, _ = panel_ref.shape
    half = twist_ref.shape[1]

    @pl.loop(0, count)
    def _(index):
        values = panel_ref[:, index].reshape(sources * steps, INNER)
        outer_stage(values, first_ref, twist_ref, mixed, index, count)

    channels = min(half, 32)

    @pl.loop(0, half // channels)
    def _(tile):
        start = pl.multiple_of(tile * channels, channels)
        rows = mixed_rows(mixed, start * count, channels * count)
        result = inner_stage(rows, gain_ref[pl.ds(start, channels), :], inner_ref, back_ref)
        out_ref[pl.ds(start, channels)] = result.reshape(channels, count, 2 * INNER).astype(out_ref.dtype)

    out_ref[0] = edge_stage(mixed_rows(mixed, 0, count), edge_ref).astype(out_ref.dtype)


def filter_columns(series, tables, gains):
    first, twist, inner, back = tables
    gain, edge = gains
    sources, columns, steps, _ = series.shape
    half = twist.shape[1]
    count = math.gcd(columns, 16)
    whole = lambda array: pl.BlockSpec(array.shape, lambda step: (0,) * array.ndim)
    return pl.pallas_call(
        filter_kernel,
        grid=(columns // count,),
        in_specs=[
            pl.BlockSpec((sources, count, steps, INNER), lambda step: (0, step, 0, 0)),
            *map(whole, (first, twist, inner, back, gain, edge)),
        ],
        out_specs=pl.BlockSpec((half, count, 2 * INNER), lambda step: (0, step, 0)),
        out_shape=jax.ShapeDtypeStruct((half, columns, 2 * INNER), jnp.bfloat16),
        scratch_shapes=[pltpu.VMEM((2 * INNER // LANES, half * count, LANES), jnp.float32)],
        compiler_params=pltpu.CompilerParams(vmem_limit_bytes=VMEM_BYTES),
    )(series, first, twist, inner, back, gain, edge)


def gram_kernel(left_ref, right_ref, out_ref, *, scale):
    step = pl.program_id(2)

    @pl.when(step == 0)
    def _():
        out_ref[...] = jnp.zeros_like(out_ref)

    out_ref[...] += lax.dot_general(
        left_ref[0], right_ref[0], (((1,), (1,)), ((), ())), preferred_element_type=jnp.float32
    )

    @pl.when(step == pl.num_programs(2) - 1)
    def _():
        out_ref[...] = out_ref[...] * scale


def gram(values, scale):
    channels, columns, depth = values.shape
    block = math.gcd(columns, 512)
    return pl.pallas_call(
        functools.partial(gram_kernel, scale=scale),
        grid=(columns // block, columns // block, channels),
        in_specs=[
            pl.BlockSpec((1, block, depth), lambda i, j, k: (k, i, 0)),
            pl.BlockSpec((1, block, depth), lambda i, j, k: (k, j, 0)),
        ],
        out_specs=pl.BlockSpec((block, block), lambda i, j, k: (i, j)),
        out_shape=jax.ShapeDtypeStruct((columns, columns), jnp.float32),
        compiler_params=pltpu.CompilerParams(vmem_limit_bytes=VMEM_BYTES),
    )(values, values)


def on_device(panel, response):
    col_rows, epoch_count = panel.shape
    tm_count = lax.axis_size("tm")
    total_len = tm_count * epoch_count
    tables = tuple(jnp.asarray(table) for table in make_tables(total_len))
    gains = gain_tables(response, total_len)
    grouped = panel.reshape(tm_count, col_rows // tm_count, epoch_count // INNER, INNER)
    series = lax.all_to_all(grouped, "tm", split_axis=0, concat_axis=0, tiled=True)
    filtered = filter_columns(series, tables, gains)
    landed = lax.all_to_all(filtered, ("col", "tm"), split_axis=0, concat_axis=1, tiled=True)
    partial_sum = gram(landed, INNER / total_len / total_len)
    summed = lax.psum_scatter(partial_sum, "col", scatter_dimension=0, tiled=True)
    return lax.psum_scatter(summed, "tm", scatter_dimension=1, tiled=True)


def solution(mesh):
    in_specs = (P("col", "tm"), P())
    out_specs = P("col", "tm")
    return jax.shard_map(
        on_device, mesh=mesh, in_specs=in_specs, out_specs=out_specs, check_vma=False
    )
```

time: 1240 us -> 521 us (0.42)
  waiting for transfers between devices: 687 us -> 203 us
  matrix products: 383 us -> 2.25 us
  blocking collectives: 99.7 us -> 188 us
  Pallas kernels: 0 us -> 84.1 us
  local copies, waits for them, and re-layouts: 35.2 us -> 20.6 us
    all_gather x1 -> x0, waiting for transfers between devices: 562 us -> none  [on_device(): lax.all_gather(whitened, 'col', axis=0, tiled=True)]
    dot_general x15 -> x2, matrix products: 383 us -> 2.25 us  [gain_tables(): blocks.append(jnp.dot(scaled, basis.T, precision=lax.Precision.HIGHEST))]
    all_to_all x1, blocking collectives: 99.7 us -> 188 us  [on_device(): lax.all_to_all(filtered, ('col', 'tm'), split_axis=0, concat_axis=1, tile...]
    pallas_call x0 -> x2, Pallas kernels: none -> 84.1 us  [the longest x1 52.4 us: filter_columns(): pl.pallas_call(filter_kernel, grid=(columns // count,), in_specs=[pl.Bloc...]
    reduce_scatter x1 -> x2, waiting for transfers between devices: 34.4 us -> 116 us  [the longest x1 76.1 us: on_device(): lax.psum_scatter(partial_sum, 'col', scatter_dimension=0, tiled=True)]
    convert_element_type x2 -> x0, local copies, waits for them, and re-layouts: 24.7 us -> none  [whiten_series(): result.reshape(block_count, item_count, block_len).astype(jnp.bfloat16)]
  transfers between devices with their start and end apart: 3 -> 3, of which waited for: 3 -> 3; matrix products, arithmetic and copies ran while one was open for 0% -> 1% of each run, Pallas kernels for 0% -> 0%
where the time goes in v1:
time: 521 us; the launch traced here: 520 us
  waiting for transfers between devices  203 us (39%)
  blocking collectives  188 us (36%)
  Pallas kernels  84.1 us (16%)
  local copies, waits for them, and re-layouts  20.6 us (4%)
  between operations  13.6 us (3%)
  starting transfers between devices  5.38 us (1%)
    all_to_all x1, blocking collectives, on_device(): lax.all_to_all(filtered, ('col', 'tm'), split_axis=0, concat_axis=1, tile...  188 us
    all_to_all x1, waiting for transfers between devices, on_device(): lax.all_to_all(grouped, 'tm', split_axis=0, concat_axis=0, tiled=True)  86.8 us
    reduce_scatter x1, waiting for transfers between devices, on_device(): lax.psum_scatter(partial_sum, 'col', scatter_dimension=0, tiled=True)  76.1 us
    pallas_call x1, Pallas kernels, filter_columns(): pl.pallas_call(filter_kernel, grid=(columns // count,), in_specs=[pl.Bloc...  52.4 us
    reduce_scatter x1, waiting for transfers between devices, on_device(): return lax.psum_scatter(summed, 'tm', scatter_dimension=1, tiled=True)  40 us
    pallas_call x1, Pallas kernels, gram(): pl.pallas_call(functools.partial(gram_kernel, scale=scale), grid=(columns...  31.7 us
    unnamed x15, local copies, waits for them, and re-layouts  11.2 us
  transfers between devices with their start and end apart: 3, of which 3 were waited for; matrix products, arithmetic and copies ran while one was open for 1% of the time, Pallas kernels for 0%

profile of v1, /device:TPU:0, one launch (start us, length us, event | category | flops | bytes accessed | tf_op | source)
XLA Modules:
  0.0 519.6 jit_solution(8559455773639955501)
XLA Ops:
  6.5 9.4 %copy.16 = bf16[32,8,64,256]{3,2,1,0:T(8,128)(2,1)} copy(bf16[32,8,64,256]{3,1,2,0:T(8,128)(2,1)} %bitcast.27) | data formatting | bytes 16777216
  15.9 5.3 %all-to-all-start = ((bf16[8,32,64,256]{3,2,1,0:T(8,128)(2,1)}), bf16[8,32,64,256]{3,2,1,0:T(8,128)(2,1)}, u32[]{:S(2)}, u32[]{:S(2)}) async-start(bf16[8,32,64,256]{3,2,1,0:T(8,128)(2,1)} %bitcast.25), calls=%async_computation | async-start | bytes 16777216 | tf_op jit(solution)/shard_map/all_to_all | solution.py:180
  21.3 0.2 slice.16
  21.5 0.5 slice.15
  22.0 0.7 reverse
  22.7 0.2 slice.30
  22.9 0.9 fusion.1
  23.8 0.1 reshape.83
  23.9 0.1 copy.14
  24.1 0.2 tile.12
  24.3 0.8 copy.17
  25.1 0.1 fusion.9
  25.3 1.6 fusion.2
  27.0 0.6 fusion.4
  27.7 0.1 subtract_convert_fusion
  27.8 0.1 fusion
  27.9 1.1 pad_maximum_fusion.1.edge_ref
  29.0 86.8 %all-to-all-done.panel_ref = bf16[8,32,64,256]{3,2,1,0:T(8,128)(2,1)} async-done(((bf16[8,32,64,256]{3,2,1,0:T(8,128)(2,1)}), bf16[8,32,64,256]{3,2,1,0:T(8,128)(2,1)}, u32[]{:S(2)}, u32[]{:S(2)}) %all-to-all-start) | async-done | bytes 8388640 | tf_op jit(solution)/shard_map/all_to_all | solution.py:180
  115.7 52.4 %shard_map.100 = bf16[256,32,512]{2,1,0:T(8,128)(2,1)} custom-call(bf16[8,32,64,256]{3,2,1,0:T(8,128)(2,1)} %all-to-all-done.panel_ref, bf16[2,512,512]{2,1,0:T(8,128)(2,1)} %constant.26.clone.first_ref, f32[2,256,256]{2,1,0:T(8,128)} %constant.27.clone.twist_ref, bf16[2,512,512]{2,1,0:T(8,128)(2,1)} %constant.28.clone.inner_ref, ...), custom_call_target="tpu_custom_call" | custom-call | tf_op jit(solution)/shard_map/pallas_call | solution.py:127
  168.1 188.4 %all_to_all.23 = bf16[256,32,512]{2,1,0:T(8,128)(2,1)} all-to-all(bf16[256,32,512]{2,1,0:T(8,128)(2,1)} %shard_map.100), channel_id=1, replica_groups=mesh['tm'=8,'col'=4] {'col','tm'}, dimensions={0} | all-to-all | bytes 16777216 | tf_op jit(solution)/shard_map/all_to_all | solution.py:182
  356.5 8.3 %copy.15 = bf16[32,8,32,512]{3,2,0,1:T(8,128)(2,1)} copy(bf16[32,8,32,512]{3,2,1,0:T(8,128)(2,1)} %bitcast.26) | data formatting | bytes 16777216 | tf_op jit(solution)/shard_map/all_to_all | solution.py:182
  364.8 31.7 %shard_map.101 = f32[1024,1024]{1,0:T(8,128)} custom-call(bf16[8,1024,512]{2,1,0:T(8,128)(2,1)} %bitcast.23, bf16[8,1024,512]{2,1,0:T(8,128)(2,1)} %bitcast.24), custom_call_target="tpu_custom_call" | custom-call | tf_op jit(solution)/shard_map/pallas_call | solution.py:160
  396.6 76.1 %reduce-scatter.3.cloned.1.call-done = f32[256,1024]{1,0:T(8,128)} async-done(((f32[1024,1024]{1,0:T(8,128)}), f32[256,1024]{1,0:T(8,128)}) %reduce-scatter.3.cloned.1.call-update) | async-done | bytes 1048592 | tf_op jit(solution)/shard_map/reduce_scatter | solution.py:184
  472.7 40.0 %reduce-scatter.5.cloned.1.call-done = f32[256,128]{1,0:T(8,128)} async-done(((f32[256,1024]{1,0:T(8,128)}), f32[256,128]{1,0:T(8,128)}) %reduce-scatter.5.cloned.1.call-update) | async-done | bytes 131088 | tf_op jit(solution)/shard_map/reduce_scatter | solution.py:185
  (18 shorter events, 0.3 us)
Async XLA Ops:
  15.9 5.4 %copy-start = (f32[131072]{0:T(1024)S(1)}, f32[131072]{0:T(1024)}, u32[]{:S(2)}) copy-start(f32[131072]{0:T(1024)} %param.11) | copy-start | bytes 1572868
  15.9 99.8 %all-to-all-start = ((bf16[8,32,64,256]{3,2,1,0:T(8,128)(2,1)}), bf16[8,32,64,256]{3,2,1,0:T(8,128)(2,1)}, u32[]{:S(2)}, u32[]{:S(2)}) async-start(bf16[8,32,64,256]{3,2,1,0:T(8,128)(2,1)} %bitcast.25), calls=%async_computation | async-start | bytes 16777216 | tf_op jit(solution)/shard_map/all_to_all | solution.py:180
  21.2 4.0 copy-start.3
  21.2 5.8 %copy-start.1 = (f32[512,256]{1,0:T(8,128)S(1)}, f32[512,256]{1,0:T(8,128)}, u32[]{:S(2)}) copy-start(f32[512,256]{1,0:T(8,128)} %constant.31.clone) | copy-start | bytes 1572868
  21.2 5.8 %copy-start.2 = (f32[256,512]{1,0:T(8,128)S(1)}, f32[256,512]{1,0:T(8,128)}, u32[]{:S(2)}) copy-start(f32[256,512]{1,0:T(8,128)} %constant.30.clone) | copy-start | bytes 1572868
  21.2 451.5 %reduce-scatter.3.cloned.1.call-start = ((), (), s32[]{:S(2)}) async-start(), calls=%async_computation.4 | async-start | bytes 5242880 | tf_op jit(solution)/shard_map/reduce_scatter | solution.py:184
  396.5 116.3 %reduce-scatter.5.cloned.1.call-start = ((), (), s32[]{:S(2)}) async-start(), calls=%async_computation.5 | async-start | bytes 1179648 | tf_op jit(solution)/shard_map/reduce_scatter | solution.py:185
Sparse Core Ops, SparseCore 0:
  396.6 76.0 reduce-scatter.2
  476.2 36.5 reduce-scatter.4

commit v2 on v1

--- a/solution.py
+++ b/solution.py
@@ -96,78 +96,187 @@
     return product(rows, edge[0]) + product(rows, edge[1])
 
 
-def filter_kernel(panel_ref, first_ref, twist_ref, inner_ref, back_ref, gain_ref, edge_ref, out_ref, mixed):
-    sources, count, steps, _ = panel_ref.shape
+MESH = pl.DeviceIdType.MESH
+
+
+def whiten_gram_kernel(
+    panel_ref, first_ref, twist_ref, inner_ref, back_ref, gain_ref, edge_ref, out_ref,
+    series, mixed, staged, landed, send_in, recv_in, send_out, recv_out, local_sem,
+    *, tm_count, col_count, scale,
+):
+    my_tm, my_col = lax.axis_index("tm"), lax.axis_index("col")
+    me = my_col * tm_count + my_tm
+    devices = tm_count * col_count
+    chunks, _, count, steps, _ = series.shape
     half = twist_ref.shape[1]
-
-    @pl.loop(0, count)
-    def _(index):
-        values = panel_ref[:, index].reshape(sources * steps, INNER)
-        outer_stage(values, first_ref, twist_ref, mixed, index, count)
-
-    channels = min(half, 32)
-
-    @pl.loop(0, half // channels)
-    def _(tile):
-        start = pl.multiple_of(tile * channels, channels)
-        rows = mixed_rows(mixed, start * count, channels * count)
-        result = inner_stage(rows, gain_ref[pl.ds(start, channels), :], inner_ref, back_ref)
-        out_ref[pl.ds(start, channels)] = result.reshape(channels, count, 2 * INNER).astype(out_ref.dtype)
-
-    out_ref[0] = edge_stage(mixed_rows(mixed, 0, count), edge_ref).astype(out_ref.dtype)
-
-
-def filter_columns(series, tables, gains):
+    share = half // devices
+
+    barrier = pltpu.get_barrier_semaphore()
+
+    @pl.loop(1, devices)
+    def _(offset):
+        peer = lax.rem(me + offset, devices)
+        there = {"tm": lax.rem(peer, tm_count), "col": peer // tm_count}
+        pl.semaphore_signal(barrier, inc=1, device_id=there, device_id_type=MESH)
+
+    pl.semaphore_wait(barrier, devices - 1)
+
+    def copy_in(chunk, target, sender):
+        return pltpu.make_async_remote_copy(
+            src_ref=panel_ref.at[target, pl.ds(chunk * count, count)],
+            dst_ref=series.at[chunk, sender],
+            send_sem=send_in.at[chunk, target],
+            recv_sem=recv_in.at[chunk, sender],
+            device_id={"tm": target, "col": my_col},
+            device_id_type=MESH,
+        )
+
+    def keep_in(chunk):
+        return pltpu.make_async_copy(
+            panel_ref.at[my_tm, pl.ds(chunk * count, count)], series.at[chunk, my_tm], local_sem.at[0, chunk]
+        )
+
+    def copy_out(chunk, target, sender):
+        return pltpu.make_async_remote_copy(
+            src_ref=staged.at[chunk, pl.ds(target * share, share)],
+            dst_ref=landed.at[:, sender, chunk],
+            send_sem=send_out.at[chunk, target],
+            recv_sem=recv_out.at[chunk, sender],
+            device_id={"tm": lax.rem(target, tm_count), "col": target // tm_count},
+            device_id_type=MESH,
+        )
+
+    def keep_out(chunk):
+        return pltpu.make_async_copy(
+            staged.at[chunk, pl.ds(me * share, share)], landed.at[:, me, chunk], local_sem.at[1, chunk]
+        )
+
+    def start_in(chunk):
+        @pl.loop(1, tm_count)
+        def _(offset):
+            copy_in(chunk, lax.rem(my_tm + offset, tm_count), my_tm).start()
+
+        keep_in(chunk).start()
+
+    start_in(0)
+    channels = max(share, min(half, 32))
+    targets = channels // share
+    tiles = half // channels
+
+    @pl.loop(0, chunks)
+    def _(chunk):
+        @pl.loop(1, tm_count)
+        def _(offset):
+            peer = lax.rem(my_tm + offset, tm_count)
+            copy_in(chunk, peer, peer).wait_recv()
+
+        keep_in(chunk).wait()
+
+        @pl.when(chunk + 1 < chunks)
+        def _():
+            start_in(chunk + 1)
+
+        @pl.loop(0, count)
+        def _(index):
+            values = series[chunk, :, index].reshape(tm_count * steps, INNER)
+            outer_stage(values, first_ref, twist_ref, mixed, index, count)
+
+        @pl.loop(0, tiles)
+        def _(turn):
+            tile = lax.rem((my_col + 1) * (tiles // col_count) + turn, tiles)
+            start = pl.multiple_of(tile * channels, channels)
+            rows = mixed_rows(mixed, start * count, channels * count)
+            result = inner_stage(rows, gain_ref[pl.ds(start, channels), :], inner_ref, back_ref)
+            staged[chunk, pl.ds(start, channels)] = result.reshape(channels, count, 2 * INNER).astype(
+                staged.dtype
+            )
+
+            @pl.when(tile == 0)
+            def _():
+                staged[chunk, 0] = edge_stage(mixed_rows(mixed, 0, count), edge_ref).astype(staged.dtype)
+
+            @pl.loop(0, targets)
+            def _(place):
+                target = tile * targets + lax.rem(place + my_tm, targets)
+
+                @pl.when(target != me)
+                def _():
+                    copy_out(chunk, target, me).start()
+
+                @pl.when(target == me)
+                def _():
+                    keep_out(chunk).start()
+
+    @pl.loop(0, chunks)
+    def _(chunk):
+        @pl.loop(1, devices)
+        def _(offset):
+            peer = lax.rem(me + offset, devices)
+            copy_out(chunk, peer, peer).wait_recv()
+
+        keep_out(chunk).wait()
+
+    width = out_ref.shape[2]
+    col_rows = tm_count * chunks * count
+    parts = col_rows // width
+
+    @pl.loop(0, col_count * col_count)
+    def _(block):
+        i, j = block // col_count, lax.rem(block, col_count)
+        total = jnp.zeros((col_rows, col_rows), jnp.float32)
+        for channel in range(share):
+            left = landed[channel, pl.ds(i * tm_count, tm_count)].reshape(col_rows, 2 * INNER)
+            right = landed[channel, pl.ds(j * tm_count, tm_count)].reshape(col_rows, 2 * INNER)
+            total = total + lax.dot_general(
+                left, right, (((1,), (1,)), ((), ())), preferred_element_type=jnp.float32
+            )
+        total = total * scale
+        for part in range(parts):
+            out_ref[j * parts + part, pl.ds(pl.multiple_of(i * col_rows, col_rows), col_rows), :] = total[
+                :, part * width : (part + 1) * width
+            ]
+
+    @pl.loop(0, chunks)
+    def _(chunk):
+        @pl.loop(1, tm_count)
+        def _(offset):
+            copy_in(chunk, lax.rem(my_tm + offset, tm_count), my_tm).wait_send()
+
+        @pl.loop(1, devices)
+        def _(offset):
+            copy_out(chunk, lax.rem(me + offset, devices), me).wait_send()
+
+
+def whiten_gram(grouped, tables, gains, col_count, scale):
     first, twist, inner, back = tables
     gain, edge = gains
-    sources, columns, steps, _ = series.shape
+    tm_count, per_device, steps, _ = grouped.shape
     half = twist.shape[1]
-    count = math.gcd(columns, 16)
-    whole = lambda array: pl.BlockSpec(array.shape, lambda step: (0,) * array.ndim)
+    count = math.gcd(per_device, 16)
+    chunks = per_device // count
+    devices = tm_count * col_count
+    columns = devices * per_device
+    vmem = pl.BlockSpec(memory_space=pltpu.VMEM)
     return pl.pallas_call(
-        filter_kernel,
-        grid=(columns // count,),
-        in_specs=[
-            pl.BlockSpec((sources, count, steps, INNER), lambda step: (0, step, 0, 0)),
-            *map(whole, (first, twist, inner, back, gain, edge)),
+        functools.partial(whiten_gram_kernel, tm_count=tm_count, col_count=col_count, scale=scale),
+        in_specs=[pl.BlockSpec(memory_space=pl.ANY)] + [vmem] * 6,
+        out_specs=vmem,
+        out_shape=jax.ShapeDtypeStruct((tm_count, columns, columns // tm_count), jnp.float32),
+        scratch_shapes=[
+            pltpu.VMEM((chunks, tm_count, count, steps, INNER), jnp.bfloat16),
+            pltpu.VMEM((2 * INNER // LANES, half * count, LANES), jnp.float32),
+            pltpu.VMEM((chunks, half, count, 2 * INNER), jnp.bfloat16),
+            pltpu.VMEM((half // devices, devices, chunks, count, 2 * INNER), jnp.bfloat16),
+            pltpu.SemaphoreType.DMA((chunks, tm_count)),
+            pltpu.SemaphoreType.DMA((chunks, tm_count)),
+            pltpu.SemaphoreType.DMA((chunks, devices)),
+            pltpu.SemaphoreType.DMA((chunks, devices)),
+            pltpu.SemaphoreType.DMA((2, chunks)),
         ],
-        out_specs=pl.BlockSpec((half, count, 2 * INNER), lambda step: (0, step, 0)),
-        out_shape=jax.ShapeDtypeStruct((half, columns, 2 * INNER), jnp.bfloat16),
-        scratch_shapes=[pltpu.VMEM((2 * INNER // LANES, half * count, LANES), jnp.float32)],
-        compiler_params=pltpu.CompilerParams(vmem_limit_bytes=VMEM_BYTES),
-    )(series, first, twist, inner, back, gain, edge)
-
-
-def gram_kernel(left_ref, right_ref, out_ref, *, scale):
-    step = pl.program_id(2)
-
-    @pl.when(step == 0)
-    def _():
-        out_ref[...] = jnp.zeros_like(out_ref)
-
-    out_ref[...] += lax.dot_general(
-        left_ref[0], right_ref[0], (((1,), (1,)), ((), ())), preferred_element_type=jnp.float32
-    )
-
-    @pl.when(step == pl.num_programs(2) - 1)
-    def _():
-        out_ref[...] = out_ref[...] * scale
-
-
-def gram(values, scale):
-    channels, columns, depth = values.shape
-    block = math.gcd(columns, 512)
-    return pl.pallas_call(
-        functools.partial(gram_kernel, scale=scale),
-        grid=(columns // block, columns // block, channels),
-        in_specs=[
-            pl.BlockSpec((1, block, depth), lambda i, j, k: (k, i, 0)),
-            pl.BlockSpec((1, block, depth), lambda i, j, k: (k, j, 0)),
-        ],
-        out_specs=pl.BlockSpec((block, block), lambda i, j, k: (i, j)),
-        out_shape=jax.ShapeDtypeStruct((columns, columns), jnp.float32),
-        compiler_params=pltpu.CompilerParams(vmem_limit_bytes=VMEM_BYTES),
-    )(values, values)
+        compiler_params=pltpu.CompilerParams(
+            collective_id=0, has_side_effects=True, vmem_limit_bytes=VMEM_BYTES
+        ),
+    )(grouped, first, twist, inner, back, gain, edge)
 
 
 def on_device(panel, response):
@@ -177,12 +286,11 @@
     tables = tuple(jnp.asarray(table) for table in make_tables(total_len))
     gains = gain_tables(response, total_len)
     grouped = panel.reshape(tm_count, col_rows // tm_count, epoch_count // INNER, INNER)
-    series = lax.all_to_all(grouped, "tm", split_axis=0, concat_axis=0, tiled=True)
-    filtered = filter_columns(series, tables, gains)
-    landed = lax.all_to_all(filtered, ("col", "tm"), split_axis=0, concat_axis=1, tiled=True)
-    partial_sum = gram(landed, INNER / total_len / total_len)
-    summed = lax.psum_scatter(partial_sum, "col", scatter_dimension=0, tiled=True)
-    return lax.psum_scatter(summed, "tm", scatter_dimension=1, tiled=True)
+    col_count = lax.axis_size("col")
+    partial_sum = whiten_gram(grouped, tables, gains, col_count, INNER / total_len / total_len)
+    across = lax.all_to_all(partial_sum, "tm", split_axis=0, concat_axis=0, tiled=True)
+    summed = jnp.sum(across, axis=0).reshape(col_count, col_rows, -1)
+    return jnp.sum(lax.all_to_all(summed, "col", split_axis=0, concat_axis=0, tiled=True), axis=0)
 
 
 def solution(mesh):

time: 521 us -> 355 us (0.68)
  waiting for transfers between devices: 203 us -> 0 us
  Pallas kernels: 84.1 us -> 229 us
  blocking collectives: 188 us -> 102 us
  between operations: 13.6 us -> 0.15 us
  local copies, waits for them, and re-layouts: 20.6 us -> 14.2 us
  starting transfers between devices: 5.38 us -> 0 us
    pallas_call x2 -> x1, Pallas kernels: 84.1 us -> 229 us  [whiten_gram(): pl.pallas_call(functools.partial(whiten_gram_kernel, tm_count=tm_count, c...]
    reduce_scatter x2 -> x0, waiting for transfers between devices: 116 us -> none  [the longest x1 76.1 us: on_device(): lax.psum_scatter(partial_sum, 'col', scatter_dimension=0, tiled=True)]
    all_to_all x1 -> x0, waiting for transfers between devices: 86.8 us -> none  [on_device(): lax.all_to_all(grouped, 'tm', split_axis=0, concat_axis=0, tiled=True)]
    all_to_all x1 -> x2, blocking collectives: 188 us -> 102 us  [the longest x1 64.2 us: on_device(): lax.all_to_all(partial_sum, 'tm', split_axis=0, concat_axis=0, tiled=True)]
    all_to_all x1 -> x0, local copies, waits for them, and re-layouts: 8.27 us -> none  [on_device(): lax.all_to_all(filtered, ('col', 'tm'), split_axis=0, concat_axis=1, tile...]
    all_to_all x1 -> x0, starting transfers between devices: 5.3 us -> none  [on_device(): lax.all_to_all(grouped, 'tm', split_axis=0, concat_axis=0, tiled=True)]
    unnamed x15 -> x11, local copies, waits for them, and re-layouts: 11.2 us -> 11.1 us
  transfers between devices with their start and end apart: 3 -> 0, of which waited for: 3 -> 0; matrix products, arithmetic and copies ran while one was open for 1% -> 0% of each run, Pallas kernels for 0% -> 0%
where the time goes in v2:
time: 355 us
  Pallas kernels  229 us (65%)
  blocking collectives  102 us (29%)
  local copies, waits for them, and re-layouts  14.2 us (4%)
  other arithmetic  6.53 us (2%)
    pallas_call x1, Pallas kernels, whiten_gram(): pl.pallas_call(functools.partial(whiten_gram_kernel, tm_count=tm_count, c...  229 us
    all_to_all x1, blocking collectives, on_device(): lax.all_to_all(partial_sum, 'tm', split_axis=0, concat_axis=0, tiled=True)  64.2 us
    all_to_all x1, blocking collectives, on_device(): lax.all_to_all(summed, 'col', split_axis=0, concat_axis=0, tiled=True)  38.1 us
    unnamed x11, local copies, waits for them, and re-layouts  11.1 us

profile of v2, /device:TPU:0, one launch (start us, length us, event | category | flops | bytes accessed | tf_op | source)
XLA Modules:
  0.0 354.6 jit_solution(16714680620094343038)
XLA Ops:
  0.0 0.0 copy-start.1
  0.0 1.3 slice.15
  1.3 1.2 slice.16
  2.5 0.7 reverse
  3.2 0.2 slice.30
  3.5 1.9 fusion.1
  5.4 0.1 reshape.86
  5.5 0.1 fusion.9
  5.7 1.8 fusion.2
  7.5 0.0 copy-done
  7.6 0.0 copy-done.1
  7.6 0.6 fusion.4
  8.2 0.1 subtract_convert_fusion
  8.4 0.1 fusion
  8.4 0.1 copy.13
  8.6 0.2 tile.12
  8.8 0.8 copy.15
  9.6 9.4 %copy.14 = bf16[32,8,64,256]{3,2,1,0:T(8,128)(2,1)} copy(bf16[32,8,64,256]{3,1,2,0:T(8,128)(2,1)} %bitcast.21) | data formatting | bytes 16777216
  19.0 1.1 pad_maximum_fusion.1.edge_ref
  20.1 229.0 %shard_map.100 = f32[8,1024,128]{2,1,0:T(8,128)} custom-call(bf16[8,32,64,256]{3,2,1,0:T(8,128)(2,1)} %bitcast.20, bf16[2,512,512]{2,1,0:T(8,128)(2,1)} %constant.27.clone.first_ref, f32[2,256,256]{2,1,0:T(8,128)} %constant.28.clone.twist_ref, bf16[2,512,512]{2,1,0:T(8,128)(2,1)} %constant.29.clone.inner_ref, bf16[2,512,512]{2,1,0:T(8,128)(2,1)} %constant.30.clone.back_ref, ...), custom_call_target="tpu_custom_call" | custom-call | tf_op jit(solution)/shard_map/pallas_call | solution.py:260
  249.1 64.2 %all_to_all.10 = f32[8,1024,128]{2,1,0:T(8,128)} all-to-all(f32[8,1024,128]{2,1,0:T(8,128)} %shard_map.100), channel_id=1, replica_groups=mesh['tm'=8,'col'=4] {'tm'}, dimensions={0} | all-to-all | bytes 8388608 | tf_op jit(solution)/shard_map/all_to_all | solution.py:291
  313.3 2.4 reduce_sum.18
  315.8 38.1 %all_to_all.11 = f32[4,256,128]{2,1,0:T(8,128)S(1)} all-to-all(f32[4,256,128]{2,1,0:T(8,128)S(1)} %bitcast.23), channel_id=1, replica_groups=mesh['tm'=8,'col'=4] {'col'}, dimensions={0} | all-to-all | bytes 1048576 | tf_op jit(solution)/shard_map/all_to_all | solution.py:293
  353.9 0.7 reduce_sum.19
  (7 shorter events, 0.1 us)
Async XLA Ops:
  0.0 7.5 %copy-start = (f32[512,256]{1,0:T(8,128)S(1)}, f32[512,256]{1,0:T(8,128)}, u32[]{:S(2)}) copy-start(f32[512,256]{1,0:T(8,128)} %constant.32.clone) | copy-start | bytes 1572868
  0.0 7.6 %copy-start.1 = (f32[256,512]{1,0:T(8,128)S(1)}, f32[256,512]{1,0:T(8,128)}, u32[]{:S(2)}) copy-start(f32[256,512]{1,0:T(8,128)} %constant.31.clone) | copy-start | bytes 1572868

commit v3 on v2

--- a/solution.py
+++ b/solution.py
@@ -11,6 +11,7 @@
 
 INNER = 256
 LANES = 128
+PAIR = 2
 VMEM_BYTES = 58 * 1024 * 1024
 
 
@@ -101,7 +102,9 @@
 
 def whiten_gram_kernel(
     panel_ref, first_ref, twist_ref, inner_ref, back_ref, gain_ref, edge_ref, out_ref,
-    series, mixed, staged, landed, send_in, recv_in, send_out, recv_out, local_sem,
+    series, mixed, staged, landed, partial, pair_land, plane_land, summed, line_land,
+    send_in, recv_in, send_out, recv_out, local_sem,
+    send_pair, recv_pair, send_plane, recv_plane, send_line, recv_line,
     *, tm_count, col_count, scale,
 ):
     my_tm, my_col = lax.axis_index("tm"), lax.axis_index("col")
@@ -216,25 +219,108 @@
 
         keep_out(chunk).wait()
 
-    width = out_ref.shape[2]
-    col_rows = tm_count * chunks * count
+    col_rows, width = out_ref.shape
     parts = col_rows // width
-
-    @pl.loop(0, col_count * col_count)
-    def _(block):
-        i, j = block // col_count, lax.rem(block, col_count)
-        total = jnp.zeros((col_rows, col_rows), jnp.float32)
-        for channel in range(share):
-            left = landed[channel, pl.ds(i * tm_count, tm_count)].reshape(col_rows, 2 * INNER)
-            right = landed[channel, pl.ds(j * tm_count, tm_count)].reshape(col_rows, 2 * INNER)
-            total = total + lax.dot_general(
-                left, right, (((1,), (1,)), ((), ())), preferred_element_type=jnp.float32
-            )
-        total = total * scale
-        for part in range(parts):
-            out_ref[j * parts + part, pl.ds(pl.multiple_of(i * col_rows, col_rows), col_rows), :] = total[
-                :, part * width : (part + 1) * width
-            ]
+    chips = tm_count // PAIR
+    my_chip, my_core = my_tm // PAIR, lax.rem(my_tm, PAIR)
+    other_core = PAIR - 1 - my_core
+
+    def pair_copy(row):
+        return pltpu.make_async_remote_copy(
+            src_ref=partial.at[row, other_core],
+            dst_ref=pair_land.at[row],
+            send_sem=send_pair.at[row],
+            recv_sem=recv_pair.at[row],
+            device_id={"tm": my_chip * PAIR + other_core, "col": my_col},
+            device_id_type=MESH,
+        )
+
+    def plane_copy(row, target, sender):
+        return pltpu.make_async_remote_copy(
+            src_ref=partial.at[row, my_core, target],
+            dst_ref=plane_land.at[row, sender],
+            send_sem=send_plane.at[row, target],
+            recv_sem=recv_plane.at[row, sender],
+            device_id={"tm": target * PAIR + my_core, "col": my_col},
+            device_id_type=MESH,
+        )
+
+    def line_copy(target, sender):
+        return pltpu.make_async_remote_copy(
+            src_ref=summed.at[target],
+            dst_ref=line_land.at[sender],
+            send_sem=send_line.at[target],
+            recv_sem=recv_line.at[sender],
+            device_id={"tm": my_tm, "col": target},
+            device_id_type=MESH,
+        )
+
+    @pl.loop(0, col_count + 2)
+    def _(step):
+        @pl.when(step < col_count)
+        def _():
+            row = lax.rem(my_col + 1 + step, col_count)
+
+            @pl.loop(0, col_count)
+            def _(j):
+                total = jnp.zeros((col_rows, col_rows), jnp.float32)
+                for channel in range(share):
+                    left = landed[channel, pl.ds(row * tm_count, tm_count)].reshape(col_rows, 2 * INNER)
+                    right = landed[channel, pl.ds(j * tm_count, tm_count)].reshape(col_rows, 2 * INNER)
+                    total = total + lax.dot_general(
+                        left, right, (((1,), (1,)), ((), ())), preferred_element_type=jnp.float32
+                    )
+                total = total * scale
+                for part in range(parts):
+                    owner = j * parts + part
+                    partial[row, lax.rem(owner, PAIR), owner // PAIR] = total[:, part * width : (part + 1) * width]
+
+            pair_copy(row).start()
+
+        @pl.when((step >= 1) & (step < col_count + 1))
+        def _():
+            row = lax.rem(my_col + step, col_count)
+            pair_copy(row).wait_recv()
+            partial[row, my_core] = partial[row, my_core] + pair_land[row]
+
+            @pl.loop(1, chips)
+            def _(offset):
+                plane_copy(row, lax.rem(my_chip + offset, chips), my_chip).start()
+
+        @pl.when(step >= 2)
+        def _():
+            row = lax.rem(my_col + step - 1, col_count)
+            summed[row] = partial[row, my_core, my_chip]
+
+            @pl.loop(1, chips)
+            def _(offset):
+                peer = lax.rem(my_chip + offset, chips)
+                plane_copy(row, peer, peer).wait_recv()
+                summed[row] = summed[row] + plane_land[row, peer]
+
+            @pl.when(row != my_col)
+            def _():
+                line_copy(row, my_col).start()
+
+    out_ref[...] = summed[my_col]
+
+    @pl.loop(1, col_count)
+    def _(offset):
+        peer = lax.rem(my_col + offset, col_count)
+        line_copy(peer, peer).wait_recv()
+        out_ref[...] = out_ref[...] + line_land[peer]
+
+    @pl.loop(0, col_count)
+    def _(row):
+        pair_copy(row).wait_send()
+
+        @pl.loop(1, chips)
+        def _(offset):
+            plane_copy(row, lax.rem(my_chip + offset, chips), my_chip).wait_send()
+
+        @pl.when(row != my_col)
+        def _():
+            line_copy(row, my_col).wait_send()
 
     @pl.loop(0, chunks)
     def _(chunk):
@@ -256,22 +342,35 @@
     chunks = per_device // count
     devices = tm_count * col_count
     columns = devices * per_device
+    chips = tm_count // PAIR
+    block = (columns // col_count, columns // tm_count)
     vmem = pl.BlockSpec(memory_space=pltpu.VMEM)
     return pl.pallas_call(
         functools.partial(whiten_gram_kernel, tm_count=tm_count, col_count=col_count, scale=scale),
         in_specs=[pl.BlockSpec(memory_space=pl.ANY)] + [vmem] * 6,
         out_specs=vmem,
-        out_shape=jax.ShapeDtypeStruct((tm_count, columns, columns // tm_count), jnp.float32),
+        out_shape=jax.ShapeDtypeStruct(block, jnp.float32),
         scratch_shapes=[
             pltpu.VMEM((chunks, tm_count, count, steps, INNER), jnp.bfloat16),
             pltpu.VMEM((2 * INNER // LANES, half * count, LANES), jnp.float32),
             pltpu.VMEM((chunks, half, count, 2 * INNER), jnp.bfloat16),
             pltpu.VMEM((half // devices, devices, chunks, count, 2 * INNER), jnp.bfloat16),
+            pltpu.VMEM((col_count, PAIR, chips, *block), jnp.float32),
+            pltpu.VMEM((col_count, chips, *block), jnp.float32),
+            pltpu.VMEM((col_count, chips, *block), jnp.float32),
+            pltpu.VMEM((col_count, *block), jnp.float32),
+            pltpu.VMEM((col_count, *block), jnp.float32),
             pltpu.SemaphoreType.DMA((chunks, tm_count)),
             pltpu.SemaphoreType.DMA((chunks, tm_count)),
             pltpu.SemaphoreType.DMA((chunks, devices)),
             pltpu.SemaphoreType.DMA((chunks, devices)),
             pltpu.SemaphoreType.DMA((2, chunks)),
+            pltpu.SemaphoreType.DMA((col_count,)),
+            pltpu.SemaphoreType.DMA((col_count,)),
+            pltpu.SemaphoreType.DMA((col_count, chips)),
+            pltpu.SemaphoreType.DMA((col_count, chips)),
+            pltpu.SemaphoreType.DMA((col_count,)),
+            pltpu.SemaphoreType.DMA((col_count,)),
         ],
         compiler_params=pltpu.CompilerParams(
             collective_id=0, has_side_effects=True, vmem_limit_bytes=VMEM_BYTES
@@ -287,10 +386,7 @@
     gains = gain_tables(response, total_len)
     grouped = panel.reshape(tm_count, col_rows // tm_count, epoch_count // INNER, INNER)
     col_count = lax.axis_size("col")
-    partial_sum = whiten_gram(grouped, tables, gains, col_count, INNER / total_len / total_len)
-    across = lax.all_to_all(partial_sum, "tm", split_axis=0, concat_axis=0, tiled=True)
-    summed = jnp.sum(across, axis=0).reshape(col_count, col_rows, -1)
-    return jnp.sum(lax.all_to_all(summed, "col", split_axis=0, concat_axis=0, tiled=True), axis=0)
+    return whiten_gram(grouped, tables, gains, col_count, INNER / total_len / total_len)
 
 
 def solution(mesh):

time: 355 us -> 304 us (0.86)
  blocking collectives: 102 us -> 0 us
  Pallas kernels: 229 us -> 282 us
    all_to_all x2 -> x0, blocking collectives: 102 us -> none  [the longest x1 64.2 us: on_device(): lax.all_to_all(partial_sum, 'tm', split_axis=0, concat_axis=0, tiled=True)]
    pallas_call x1, Pallas kernels: 229 us -> 282 us  [whiten_gram(): pl.pallas_call(functools.partial(whiten_gram_kernel, tm_count=tm_count, c...]
    unnamed x11 -> x12, local copies, waits for them, and re-layouts: 11.1 us -> 12.7 us
where the time goes in v3:
time: 304 us; the launch traced here: 303 us
  Pallas kernels  282 us (93%)
  local copies, waits for them, and re-layouts  15.7 us (5%)
  other arithmetic  3.42 us (1%)
    pallas_call x1, Pallas kernels, whiten_gram(): pl.pallas_call(functools.partial(whiten_gram_kernel, tm_count=tm_count, c...  282 us
    unnamed x12, local copies, waits for them, and re-layouts  12.7 us

profile of v3, /device:TPU:0, one launch (start us, length us, event | category | flops | bytes accessed | tf_op | source)
XLA Modules:
  0.0 303.4 jit_solution(16599587884607008665)
XLA Ops:
  0.0 0.0 copy-start
  0.0 0.0 copy-start.1
  0.0 1.3 slice.15
  1.3 1.2 slice.16
  2.5 0.7 reverse
  3.2 0.2 slice.30
  3.5 1.9 fusion.1
  5.4 0.1 reshape.83
  5.5 0.1 fusion.9
  5.6 0.1 copy.12
  5.8 1.8 fusion.4
  7.6 0.0 copy-done
  7.6 0.0 copy-done.1
  7.6 0.6 fusion.2
  8.3 0.1 pad_bitcast_fusion.1
  8.4 0.2 tile.12
  8.6 0.8 copy.14
  9.4 0.1 subtract_convert_fusion
  9.5 0.1 fusion
  9.6 1.2 pad_maximum_fusion.1.edge_ref
  10.7 9.4 %copy.13 = bf16[32,8,64,256]{3,2,1,0:T(8,128)(2,1)} copy(bf16[32,8,64,256]{3,1,2,0:T(8,128)(2,1)} %bitcast.20) | data formatting | bytes 16777216
  20.1 281.7 %shard_map.100 = f32[256,128]{1,0:T(8,128)} custom-call(bf16[8,32,64,256]{3,2,1,0:T(8,128)(2,1)} %bitcast.19, bf16[2,512,512]{2,1,0:T(8,128)(2,1)} %constant.26.clone.first_ref, f32[2,256,256]{2,1,0:T(8,128)} %constant.27.clone.twist_ref, bf16[2,512,512]{2,1,0:T(8,128)(2,1)} %constant.28.clone.inner_ref, bf16[2,512,512]{2,1,0:T(8,128)(2,1)} %constant.29.clone.back_ref, ...), custom_call_target="tpu_custom_call" | custom-call | tf_op jit(solution)/shard_map/pallas_call | solution.py:348
  301.9 1.6 copy.18
  (5 shorter events, 0.1 us)
Async XLA Ops:
  0.0 7.6 %copy-start = (f32[512,256]{1,0:T(8,128)S(1)}, f32[512,256]{1,0:T(8,128)}, u32[]{:S(2)}) copy-start(f32[512,256]{1,0:T(8,128)} %constant.33.clone) | copy-start | bytes 1572868
  0.0 7.6 %copy-start.1 = (f32[256,512]{1,0:T(8,128)S(1)}, f32[256,512]{1,0:T(8,128)}, u32[]{:S(2)}) copy-start(f32[256,512]{1,0:T(8,128)} %constant.32.clone) | copy-start | bytes 1572868

commit v4 on v3

--- a/solution.py
+++ b/solution.py
@@ -36,7 +36,9 @@
     cosine, sine = np.cos(angle), np.sin(angle)
     inner = split_table(np.block([[cosine, -sine], [sine, cosine]]))
     back = split_table(np.block([[cosine, sine], [-sine, cosine]]))
-    return first, twist, inner, back
+    angle = math.pi * lane / INNER
+    turn = np.stack([np.cos(angle), np.sin(angle)]).astype(np.float32)
+    return first, twist, inner, back, turn
 
 
 def gain_tables(response, total_len):
@@ -46,20 +48,8 @@
     gain = 0.5 * (response + mirrored)
     grid = gain.reshape(INNER, outer).T
     wide = jnp.tile(grid[:half] * (math.sqrt(2.0) / INNER), (1, 2))
-    lane = np.arange(INNER)
-    blocks = []
-    for shift, channel in ((0, 0), (1, half)):
-        angle = math.pi * (lane[:, None] * (2 * lane[None, :] + shift) % (2 * INNER)) / INNER
-        basis = np.concatenate([np.cos(angle), np.sin(angle)], axis=1).astype(np.float32)
-        scaled = basis * jnp.tile(grid[channel] / INNER, 2)[None, :]
-        blocks.append(jnp.dot(scaled, basis.T, precision=lax.Precision.HIGHEST))
-    zero = jnp.zeros_like(blocks[0])
-    edge = jnp.concatenate(
-        [jnp.concatenate([blocks[0], zero], axis=1), jnp.concatenate([zero, blocks[1]], axis=1)]
-    )
-    upper = edge.astype(jnp.bfloat16)
-    lower = (edge - upper.astype(jnp.float32)).astype(jnp.bfloat16)
-    return wide, jnp.stack([upper, lower])
+    edge = jnp.tile(jnp.stack([grid[0], grid[half]]) * (1.0 / INNER), (1, 2))
+    return wide, edge
 
 
 def product(left, right):
@@ -92,16 +82,27 @@
     return product(upper, back[0]) + product(lower, back[0]) + product(upper, back[1])
 
 
-def edge_stage(values, edge):
-    rows = values.astype(jnp.bfloat16)
-    return product(rows, edge[0]) + product(rows, edge[1])
+def edge_stage(values, gain, inner, back, turn):
+    low, high = values[:, :INNER], values[:, INNER:]
+    cosine, sine = turn[0:1], turn[1:2]
+    rows = jnp.concatenate(
+        [
+            jnp.concatenate([low, jnp.zeros_like(low)], axis=1),
+            jnp.concatenate([high * cosine, -high * sine], axis=1),
+        ]
+    )
+    result = inner_stage(rows, gain, inner, back)
+    size = values.shape[0]
+    low = result[:size, :INNER]
+    high = result[size:, :INNER] * cosine - result[size:, INNER:] * sine
+    return jnp.concatenate([low, high], axis=1)
 
 
 MESH = pl.DeviceIdType.MESH
 
 
 def whiten_gram_kernel(
-    panel_ref, first_ref, twist_ref, inner_ref, back_ref, gain_ref, edge_ref, out_ref,
+    panel_ref, first_ref, twist_ref, inner_ref, back_ref, gain_ref, edge_ref, turn_ref, out_ref,
     series, mixed, staged, landed, partial, pair_land, plane_land, summed, line_land,
     send_in, recv_in, send_out, recv_out, local_sem,
     send_pair, recv_pair, send_plane, recv_plane, send_line, recv_line,
@@ -186,7 +187,10 @@
 
         @pl.loop(0, tiles)
         def _(turn):
-            tile = lax.rem((my_col + 1) * (tiles // col_count) + turn, tiles)
+            per_side = tiles // 2
+            side = lax.rem(my_col // (col_count // 2) + 1 + turn // per_side, 2)
+            shift = lax.rem(my_col, col_count // 2) * (tiles // col_count)
+            tile = side * per_side + lax.rem(turn + shift, per_side)
             start = pl.multiple_of(tile * channels, channels)
             rows = mixed_rows(mixed, start * count, channels * count)
             result = inner_stage(rows, gain_ref[pl.ds(start, channels), :], inner_ref, back_ref)
@@ -196,7 +200,9 @@
 
             @pl.when(tile == 0)
             def _():
-                staged[chunk, 0] = edge_stage(mixed_rows(mixed, 0, count), edge_ref).astype(staged.dtype)
+                staged[chunk, 0] = edge_stage(
+                    mixed_rows(mixed, 0, count), edge_ref[...], inner_ref, back_ref, turn_ref
+                ).astype(staged.dtype)
 
             @pl.loop(0, targets)
             def _(place):
@@ -334,11 +340,11 @@
 
 
 def whiten_gram(grouped, tables, gains, col_count, scale):
-    first, twist, inner, back = tables
+    first, twist, inner, back, turn = tables
     gain, edge = gains
     tm_count, per_device, steps, _ = grouped.shape
     half = twist.shape[1]
-    count = math.gcd(per_device, 16)
+    count = math.gcd(per_device, 8)
     chunks = per_device // count
     devices = tm_count * col_count
     columns = devices * per_device
@@ -347,7 +353,7 @@
     vmem = pl.BlockSpec(memory_space=pltpu.VMEM)
     return pl.pallas_call(
         functools.partial(whiten_gram_kernel, tm_count=tm_count, col_count=col_count, scale=scale),
-        in_specs=[pl.BlockSpec(memory_space=pl.ANY)] + [vmem] * 6,
+        in_specs=[pl.BlockSpec(memory_space=pl.ANY)] + [vmem] * 7,
         out_specs=vmem,
         out_shape=jax.ShapeDtypeStruct(block, jnp.float32),
         scratch_shapes=[
@@ -375,7 +381,7 @@
         compiler_params=pltpu.CompilerParams(
             collective_id=0, has_side_effects=True, vmem_limit_bytes=VMEM_BYTES
         ),
-    )(grouped, first, twist, inner, back, gain, edge)
+    )(grouped, first, twist, inner, back, gain, edge, turn)
 
 
 def on_device(panel, response):

time: 304 us -> 282 us (0.928)
  Pallas kernels: 282 us -> 263 us
    pallas_call x1, Pallas kernels: 282 us -> 263 us  [whiten_gram(): pl.pallas_call(functools.partial(whiten_gram_kernel, tm_count=tm_count, c...]
    unnamed x12 -> x7, local copies, waits for them, and re-layouts: 12.7 us -> 13.4 us
where the time goes in v4:
time: 282 us
  Pallas kernels  263 us (93%)
  local copies, waits for them, and re-layouts  16.4 us (6%)
    pallas_call x1, Pallas kernels, whiten_gram(): pl.pallas_call(functools.partial(whiten_gram_kernel, tm_count=tm_count, c...  263 us
    unnamed x7, local copies, waits for them, and re-layouts  13.4 us

profile of v4, /device:TPU:0, one launch (start us, length us, event | category | flops | bytes accessed | tf_op | source)
XLA Modules:
  0.0 281.7 jit_solution(10260980213332869945)
XLA Ops:
  0.0 1.2 slice.15
  1.2 1.2 slice.16
  2.4 0.7 reverse
  3.2 0.2 slice.24
  3.4 1.9 fusion
  5.3 0.1 reshape.29
  5.4 0.1 copy.11
  5.5 0.1 copy.10
  5.7 0.1 copy.12
  5.8 0.6 copy.15
  6.4 0.2 tile.8
  6.5 0.9 copy.14
  7.4 9.4 %copy.13 = bf16[32,8,64,256]{3,2,1,0:T(8,128)(2,1)} copy(bf16[32,8,64,256]{3,1,2,0:T(8,128)(2,1)} %bitcast.11) | data formatting | bytes 16777216
  16.8 263.4 %shard_map.73 = f32[256,128]{1,0:T(8,128)} custom-call(bf16[8,32,64,256]{3,2,1,0:T(8,128)(2,1)} %bitcast.10, bf16[2,512,512]{2,1,0:T(8,128)(2,1)} %constant.16.clone.first_ref, f32[2,256,256]{2,1,0:T(8,128)} %constant.17.clone.twist_ref, bf16[2,512,512]{2,1,0:T(8,128)(2,1)} %constant.18.clone.inner_ref, bf16[2,512,512]{2,1,0:T(8,128)(2,1)} %constant.19.clone.back_ref, ...), custom_call_target="tpu_custom_call" | custom-call | tf_op jit(solution)/shard_map/pallas_call | solution.py:354
  280.2 1.6 copy.17
  (4 shorter events, 0.1 us)

commit v5 on v4

--- a/solution.py
+++ b/solution.py
@@ -103,7 +103,7 @@
 
 def whiten_gram_kernel(
     panel_ref, first_ref, twist_ref, inner_ref, back_ref, gain_ref, edge_ref, turn_ref, out_ref,
-    series, mixed, staged, landed, partial, pair_land, plane_land, summed, line_land,
+    series, mixed, staged, landed, flat, partial, pair_land, plane_land, summed, line_land,
     send_in, recv_in, send_out, recv_out, local_sem,
     send_pair, recv_pair, send_plane, recv_plane, send_line, recv_line,
     *, tm_count, col_count, scale,
@@ -216,16 +216,29 @@
                 def _():
                     keep_out(chunk).start()
 
-    @pl.loop(0, chunks)
-    def _(chunk):
-        @pl.loop(1, devices)
-        def _(offset):
-            peer = lax.rem(me + offset, devices)
-            copy_out(chunk, peer, peer).wait_recv()
-
-        keep_out(chunk).wait()
-
     col_rows, width = out_ref.shape
+
+    @pl.loop(0, col_count)
+    def _(offset):
+        group = lax.rem(my_col + offset, col_count)
+
+        @pl.loop(0, tm_count * chunks)
+        def _(item):
+            peer, chunk = group * tm_count + item // chunks, lax.rem(item, chunks)
+
+            @pl.when(peer != me)
+            def _():
+                copy_out(chunk, peer, peer).wait_recv()
+
+            @pl.when(peer == me)
+            def _():
+                keep_out(chunk).wait()
+
+        for channel in range(share):
+            flat[channel, pl.ds(pl.multiple_of(group * col_rows, col_rows), col_rows)] = landed[
+                channel, pl.ds(group * tm_count, tm_count)
+            ].reshape(col_rows, 2 * INNER)
+
     parts = col_rows // width
     chips = tm_count // PAIR
     my_chip, my_core = my_tm // PAIR, lax.rem(my_tm, PAIR)
@@ -271,8 +284,8 @@
             def _(j):
                 total = jnp.zeros((col_rows, col_rows), jnp.float32)
                 for channel in range(share):
-                    left = landed[channel, pl.ds(row * tm_count, tm_count)].reshape(col_rows, 2 * INNER)
-                    right = landed[channel, pl.ds(j * tm_count, tm_count)].reshape(col_rows, 2 * INNER)
+                    left = flat[channel, pl.ds(pl.multiple_of(row * col_rows, col_rows), col_rows)]
+                    right = flat[channel, pl.ds(pl.multiple_of(j * col_rows, col_rows), col_rows)]
                     total = total + lax.dot_general(
                         left, right, (((1,), (1,)), ((), ())), preferred_element_type=jnp.float32
                     )
@@ -361,6 +374,7 @@
             pltpu.VMEM((2 * INNER // LANES, half * count, LANES), jnp.float32),
             pltpu.VMEM((chunks, half, count, 2 * INNER), jnp.bfloat16),
             pltpu.VMEM((half // devices, devices, chunks, count, 2 * INNER), jnp.bfloat16),
+            pltpu.VMEM((half // devices, columns, 2 * INNER), jnp.bfloat16),
             pltpu.VMEM((col_count, PAIR, chips, *block), jnp.float32),
             pltpu.VMEM((col_count, chips, *block), jnp.float32),
             pltpu.VMEM((col_count, chips, *block), jnp.float32),

time: 282 us -> 283 us (level)
  no operation moved by 1% of the time
where the time goes in v5:
time: 283 us
  Pallas kernels  265 us (94%)
  local copies, waits for them, and re-layouts  16.4 us (6%)
    pallas_call x1, Pallas kernels, whiten_gram(): pl.pallas_call(functools.partial(whiten_gram_kernel, tm_count=tm_count, c...  265 us
    unnamed x7, local copies, waits for them, and re-layouts  13.4 us

profile of v5, /device:TPU:0, one launch (start us, length us, event | category | flops | bytes accessed | tf_op | source)
XLA Modules:
  0.0 283.0 jit_solution(14013188176593740160)
XLA Ops:
  0.0 1.2 slice.15
  1.2 1.2 slice.16
  2.4 0.7 reverse
  3.2 0.2 slice.24
  3.4 1.9 fusion
  5.3 0.1 reshape.29
  5.4 0.1 copy.11
  5.5 0.1 copy.10
  5.7 0.1 copy.12
  5.8 0.6 copy.15
  6.4 0.2 tile.8
  6.5 0.9 copy.14
  7.4 9.4 %copy.13 = bf16[32,8,64,256]{3,2,1,0:T(8,128)(2,1)} copy(bf16[32,8,64,256]{3,1,2,0:T(8,128)(2,1)} %bitcast.11) | data formatting | bytes 16777216
  16.8 264.6 %shard_map.73 = f32[256,128]{1,0:T(8,128)} custom-call(bf16[8,32,64,256]{3,2,1,0:T(8,128)(2,1)} %bitcast.10, bf16[2,512,512]{2,1,0:T(8,128)(2,1)} %constant.16.clone.first_ref, f32[2,256,256]{2,1,0:T(8,128)} %constant.17.clone.twist_ref, bf16[2,512,512]{2,1,0:T(8,128)(2,1)} %constant.18.clone.inner_ref, bf16[2,512,512]{2,1,0:T(8,128)(2,1)} %constant.19.clone.back_ref, ...), custom_call_target="tpu_custom_call" | custom-call | tf_op jit(solution)/shard_map/pallas_call | solution.py:367
  281.4 1.6 copy.17
  (4 shorter events, 0.1 us)
